TPU v7x, 512 devices: a whole 4x4x16 slice. The times are simulated.
512 devices in a mesh: prow: 32 (over x, y, core), pcol: 16 (over z).
Axes of the slice: x: 4, y: 4, z: 16, core: 2. Of those that a mesh axis runs over, the one named last changes fastest.
Arguments:
- matrix: float32 [16384, 8192], P('prow', 'pcol'), may hold values from -6 to 6
- pivots: int32 [4, 256], replicated, may hold values from 256 to 16383, as said below
- block_inverses: bfloat16 [4, 256, 256], replicated, may hold values from -1 to 1, as said below
Outputs:
- factored: float32 [16384, 8192], P('prow', 'pcol')
Inputs may be any that keep to these rules, and one draw needn't show every extreme that they name: Within step k the 256 pivots pivots[k, j] are distinct rows at or after (k + 1) * 256. Taking together the rows of all row blocks b with the same b mod 32, each such set holds at most 16 of one step's pivots, and in every step one set holds exactly 16. `block_inverses`: the diagonal of every block is positive.
All inputs are finite; a program needn't handle non-finite values.
Results may differ from a plain program's by a relative error of at most 0.0003.
Values sent between devices are 32-bit elements; how exact they have to be, the bound alone decides.
A program may use at most 64 MiB of HBM per device.

v0:
```python
import jax
import jax.numpy as jnp
from jax import lax
from jax.sharding import PartitionSpec as P


def spread(value, axis, root):
    mine = lax.axis_index(axis) == root
    return lax.psum(jnp.where(mine, value, jnp.zeros_like(value)), axis)


def exact_dot(left, right):
    return jnp.dot(left, right, precision=lax.Precision.HIGHEST, preferred_element_type=jnp.float32)


def per_device(matrix, pivots, block_inverses):
    grid_rows = lax.axis_size("prow")
    grid_cols = lax.axis_size("pcol")
    my_row = lax.axis_index("prow")
    my_col = lax.axis_index("pcol")
    steps_total, panel_width = pivots.shape
    local_rows, local_cols = matrix.shape
    slots = 2 * panel_width // grid_rows
    row_block = jnp.arange(local_rows, dtype=jnp.int32) // panel_width * grid_rows + my_row
    col_block = jnp.arange(local_cols, dtype=jnp.int32) // panel_width * grid_cols + my_col
    identity = jnp.eye(panel_width, dtype=jnp.float32)
    current = matrix
    for panel_step in range(steps_total):
        inverse = block_inverses[panel_step].astype(jnp.float32)
        upper_inverse = jnp.triu(inverse)
        lower_inverse = jnp.tril(inverse, -1) + identity
        pivots_now = pivots[panel_step]
        pivot_block = pivots_now // panel_width
        owners = pivot_block % grid_rows
        local_row = pivot_block // grid_rows * panel_width + pivots_now % panel_width
        onehot = (owners[:, None] == jnp.arange(grid_rows, dtype=jnp.int32)[None, :]).astype(
            jnp.int32
        )
        earlier = jnp.cumsum(onehot, axis=0) - onehot
        slot_rank = jnp.sum(earlier * onehot, axis=1)
        is_mine = owners == my_row
        slot_index = jnp.where(is_mine, slot_rank, slots)
        slot_rows = jnp.zeros((slots,), jnp.int32).at[slot_index].set(local_row, mode="drop")
        filled = jnp.zeros((slots,), jnp.bool_).at[slot_index].set(True, mode="drop")
        packed = jnp.where(filled[:, None], current[slot_rows], 0.0)
        source = owners * slots + slot_rank
        root_row = panel_step % grid_rows
        start = panel_step // grid_rows * panel_width
        leaving = spread(current[start : start + panel_width], "prow", root_row)
        target = jnp.where(is_mine, local_row, local_rows)
        swapped = current.at[target].set(leaving, mode="drop")
        gathered = lax.all_gather(packed, "prow", axis=0, tiled=True)
        raw_rows = gathered[source]
        solved = exact_dot(lower_inverse, raw_rows)
        top_final = jnp.where(col_block[None, :] > panel_step, solved, raw_rows)
        old_top = swapped[start : start + panel_width]
        swapped = swapped.at[start : start + panel_width].set(
            jnp.where(my_row == root_row, top_final, old_top)
        )
        col_start = panel_step // grid_cols * panel_width
        below_mask = row_block > panel_step
        factor = jnp.where(
            below_mask[:, None],
            exact_dot(swapped[:, col_start : col_start + panel_width], upper_inverse),
            0.0,
        )
        factor = spread(factor, "pcol", panel_step % grid_cols)
        right_rows = jnp.where((col_block > panel_step)[None, :], top_final, 0.0)
        updated = swapped - exact_dot(factor, right_rows)
        kept_panel = updated[:, col_start : col_start + panel_width]
        is_panel = (my_col == panel_step % grid_cols) & below_mask[:, None]
        current = updated.at[:, col_start : col_start + panel_width].set(
            jnp.where(is_panel, factor, kept_panel)
        )
    return current


def solution(mesh):
    placed = (P("prow", "pcol"), P(), P())
    return jax.shard_map(
        per_device, mesh=mesh, in_specs=placed, out_specs=P("prow", "pcol"), check_vma=False
    )
```

profile of v0, /device:TPU:6, one launch (start us, length us, event | category | flops | bytes accessed | tf_op | source)
XLA Modules:
  0.0 1375.9 jit_solution(17448061265797655838)
XLA Ops:
  22.6 127.4 %all-reduce.9.cloned.1.call-done = f32[256,512]{1,0:T(8,128)} async-done(((f32[256,512]{1,0:T(8,128)}), f32[256,512]{1,0:T(8,128)}) %all-reduce.9.cloned.1.call-update) | async-done | bytes 524304 | tf_op jit(solution)/shard_map/psum | solution.py:9
  150.0 2.3 scatter_fusion
  152.4 57.9 %all-gather.5.cloned.1.call-done = f32[512,512]{1,0:T(8,128)} async-done(((f32[16,512]{1,0:T(8,128)}), f32[512,512]{1,0:T(8,128)}) %all-gather.5.cloned.1.call-update) | async-done | bytes 1048592 | tf_op jit(solution)/shard_map/all_gather | solution.py:52
  210.2 2.4 gather_fusion.1
  217.1 134.5 %all-reduce.11.cloned.1.call-done = f32[512,256]{1,0:T(8,128)} async-done(((f32[512,256]{1,0:T(8,128)}), f32[512,256]{1,0:T(8,128)}) %all-reduce.11.cloned.1.call-update) | async-done | bytes 524304 | tf_op jit(solution)/shard_map/psum | solution.py:9
  358.3 129.0 %all-reduce.13.cloned.1.call-done = f32[256,512]{1,0:T(8,128)} async-done(((f32[256,512]{1,0:T(8,128)}), f32[256,512]{1,0:T(8,128)}) %all-reduce.13.cloned.1.call-update) | async-done | bytes 524304 | tf_op jit(solution)/shard_map/psum | solution.py:9
  487.3 2.5 scatter_fusion.1
  489.8 57.6 %all-gather.7.cloned.1.call-done = f32[512,512]{1,0:T(8,128)} async-done(((f32[16,512]{1,0:T(8,128)}), f32[512,512]{1,0:T(8,128)}) %all-gather.7.cloned.1.call-update) | async-done | bytes 1048592 | tf_op jit(solution)/shard_map/all_gather | solution.py:52
  547.4 2.4 gather_fusion.3
  553.6 135.1 %all-reduce.15.cloned.1.call-done = f32[512,256]{1,0:T(8,128)} async-done(((f32[512,256]{1,0:T(8,128)}), f32[512,256]{1,0:T(8,128)}) %all-reduce.15.cloned.1.call-update) | async-done | bytes 524304 | tf_op jit(solution)/shard_map/psum | solution.py:9
  688.8 2.1 convolution_subtract_fusion.2
  695.5 129.0 %all-reduce.17.cloned.1.call-done = f32[256,512]{1,0:T(8,128)} async-done(((f32[256,512]{1,0:T(8,128)}), f32[256,512]{1,0:T(8,128)}) %all-reduce.17.cloned.1.call-update) | async-done | bytes 524304 | tf_op jit(solution)/shard_map/psum | solution.py:9
  824.5 2.3 scatter_fusion.2
  826.8 57.9 %all-gather.9.cloned.1.call-done = f32[512,512]{1,0:T(8,128)} async-done(((f32[16,512]{1,0:T(8,128)}), f32[512,512]{1,0:T(8,128)}) %all-gather.9.cloned.1.call-update) | async-done | bytes 1048592 | tf_op jit(solution)/shard_map/all_gather | solution.py:52
  884.7 2.4 gather_fusion.5
  890.9 135.1 %all-reduce.19.cloned.1.call-done = f32[512,256]{1,0:T(8,128)} async-done(((f32[512,256]{1,0:T(8,128)}), f32[512,256]{1,0:T(8,128)}) %all-reduce.19.cloned.1.call-update) | async-done | bytes 524304 | tf_op jit(solution)/shard_map/psum | solution.py:9
  1026.0 2.1 convolution_subtract_fusion.1
  1032.8 129.0 %all-reduce.21.cloned.1.call-done = f32[256,512]{1,0:T(8,128)} async-done(((f32[256,512]{1,0:T(8,128)}), f32[256,512]{1,0:T(8,128)}) %all-reduce.21.cloned.1.call-update) | async-done | bytes 524304 | tf_op jit(solution)/shard_map/psum | solution.py:9
  1161.8 2.5 scatter_fusion.3
  1164.3 57.7 %all-gather.11.cloned.1.call-done = f32[512,512]{1,0:T(8,128)} async-done(((f32[16,512]{1,0:T(8,128)}), f32[512,512]{1,0:T(8,128)}) %all-gather.11.cloned.1.call-update) | async-done | bytes 1048592 | tf_op jit(solution)/shard_map/all_gather | solution.py:52
  1222.0 2.4 gather_fusion.7
  1226.7 136.6 %all-reduce.23.cloned.1.call-done = f32[512,256]{1,0:T(8,128)} async-done(((f32[512,256]{1,0:T(8,128)}), f32[512,256]{1,0:T(8,128)}) %all-reduce.23.cloned.1.call-update) | async-done | bytes 524304 | tf_op jit(solution)/shard_map/psum | solution.py:9
  1363.3 3.1 convolution_subtract_fusion
  1366.5 2.6 fusion.7
  (146 shorter events, 45.6 us)
Async XLA Ops:
  6.5 143.5 %all-reduce.9.cloned.1.call-start = ((), (), s32[]{:S(2)}) async-start(), calls=%async_computation | async-start | bytes 1048576 | tf_op jit(solution)/shard_map/psum | solution.py:9
  8.6 0.7 copy-start.5
  8.6 201.6 %all-gather.5.cloned.1.call-start = ((), (), s32[]{:S(2)}) async-start(), calls=%async_computation.1 | async-start | bytes 1081344 | tf_op jit(solution)/shard_map/all_gather | solution.py:52
  13.1 0.6 copy-start.8
  14.5 0.6 copy-start.9
  15.1 0.7 slice-start
  15.9 0.7 slice-start.1
  16.6 0.7 slice-start.2
  17.4 0.7 slice-start.3
  22.5 329.1 %all-reduce.11.cloned.1.call-start = ((), (), s32[]{:S(2)}) async-start(), calls=%async_computation.2 | async-start | bytes 1048576 | tf_op jit(solution)/shard_map/psum | solution.py:9
  152.3 60.3 %copy-start = (bf16[4,256,256]{2,1,0:T(8,128)(2,1)S(1)}, bf16[4,256,256]{2,1,0:T(8,128)(2,1)}, u32[]{:S(2)}) copy-start(bf16[4,256,256]{2,1,0:T(8,128)(2,1)} %param.21) | copy-start | bytes 1572868
  215.0 272.4 %all-reduce.13.cloned.1.call-start = ((), (), s32[]{:S(2)}) async-start(), calls=%async_computation.3 | async-start | bytes 1048576 | tf_op jit(solution)/shard_map/psum | solution.py:9
  351.6 2.1 copy-start.2
  355.4 192.0 %all-gather.7.cloned.1.call-start = ((), (), s32[]{:S(2)}) async-start(), calls=%async_computation.4 | async-start | bytes 1081344 | tf_op jit(solution)/shard_map/all_gather | solution.py:52
  358.2 330.5 %all-reduce.15.cloned.1.call-start = ((), (), s32[]{:S(2)}) async-start(), calls=%async_computation.5 | async-start | bytes 1048576 | tf_op jit(solution)/shard_map/psum | solution.py:9
  552.1 272.3 %all-reduce.17.cloned.1.call-start = ((), (), s32[]{:S(2)}) async-start(), calls=%async_computation.6 | async-start | bytes 1048576 | tf_op jit(solution)/shard_map/psum | solution.py:9
  688.8 2.1 copy-start.3
  692.6 192.1 %all-gather.9.cloned.1.call-start = ((), (), s32[]{:S(2)}) async-start(), calls=%async_computation.7 | async-start | bytes 1081344 | tf_op jit(solution)/shard_map/all_gather | solution.py:52
  695.4 330.6 %all-reduce.19.cloned.1.call-start = ((), (), s32[]{:S(2)}) async-start(), calls=%async_computation.8 | async-start | bytes 1048576 | tf_op jit(solution)/shard_map/psum | solution.py:9
  889.4 272.3 %all-reduce.21.cloned.1.call-start = ((), (), s32[]{:S(2)}) async-start(), calls=%async_computation.9 | async-start | bytes 1048576 | tf_op jit(solution)/shard_map/psum | solution.py:9
  1026.0 2.1 copy-start.1
  1029.8 192.1 %all-gather.11.cloned.1.call-start = ((), (), s32[]{:S(2)}) async-start(), calls=%async_computation.10 | async-start | bytes 1081344 | tf_op jit(solution)/shard_map/all_gather | solution.py:52
  1032.7 330.7 %all-reduce.23.cloned.1.call-start = ((), (), s32[]{:S(2)}) async-start(), calls=%async_computation.11 | async-start | bytes 1048576 | tf_op jit(solution)/shard_map/psum | solution.py:9
  1363.3 3.1 copy-start.4
  (2 other events, 1.2 us)
Sparse Core Ops, SparseCore 0:
  10.5 139.4 all-reduce.8
  153.6 56.5 all-gather.4
  215.1 136.4 all-reduce.10
  355.5 131.7 all-reduce.12
  490.8 56.5 all-gather.6
  552.3 136.4 all-reduce.14
  692.7 131.7 all-reduce.16
  828.1 56.5 all-gather.8
  889.5 136.4 all-reduce.18
  1030.0 131.7 all-reduce.20
  1165.4 56.5 all-gather.10
  1226.8 136.4 all-reduce.22
where the time goes:
time: 1380 us
  waiting for transfers between devices  1290 us (93%)
  local copies, waits for them, and re-layouts  40.8 us (3%)
  matrix products  18.6 us (1%)
  other arithmetic  15 us (1%)
  between operations  14.2 us (1%)
    psum x8, waiting for transfers between devices, spread(): return lax.psum(jnp.where(mine, value, jnp.zeros_like(value)), axis)  1060 us
    all_gather x4, waiting for transfers between devices, per_device(): gathered = lax.all_gather(packed, 'prow', axis=0, tiled=True)  231 us
  transfers between devices with their start and end apart: 12, of which 12 were waited for; matrix products, arithmetic and copies ran while one was open for 2% of the time, Pallas kernels for 0%

commit v1 on v0

v1 whole, which is shorter than its diff:
```python
import jax
import jax.numpy as jnp
from jax import lax
from jax.experimental import pallas as pl
from jax.experimental.pallas import tpu as pltpu
from jax.sharding import PartitionSpec as P

NB = 256
STEPS = 4
CAP = 16
SLOTS = STEPS * CAP
TOPS = 32
PIECE = SLOTS + TOPS
SIDE = 4
PROWS = 32
RING = 16
WIDE = 512
PAN = STEPS * NB
F32 = jnp.float32
MIB = 1024 * 1024


def prep_kernel(coord, piv_ref, a_ref, packed_ref, source_ref, slot_row_ref, slot_source_ref):
    me = coord[0].astype(F32)
    sub = lax.broadcasted_iota(jnp.int32, (NB, NB), 0)
    lane = lax.broadcasted_iota(jnp.int32, (NB, NB), 1)
    lane_row = lax.broadcasted_iota(jnp.int32, (1, NB), 1).astype(F32)
    lane_slot = lax.broadcasted_iota(jnp.int32, (NB, 128), 1).astype(F32)
    sub_slot = lax.broadcasted_iota(jnp.int32, (CAP, NB), 0).astype(F32)
    lane_wide = lax.broadcasted_iota(jnp.int32, (CAP, WIDE), 1).astype(F32)

    def column(row):
        return jnp.sum(jnp.where(sub == lane, row, 0.0), axis=1, keepdims=True)

    def pick(mask, value):
        return jnp.sum(jnp.where(mask, value, 0.0), axis=0, keepdims=True)

    def top_index(row):
        t = row.astype(jnp.int32)
        return ((t & 255) >> 3) * PIECE + SLOTS + (t >> 8) * 8 + (t & 7)

    source_ref[...] = jnp.zeros_like(source_ref)
    slot_row_ref[...] = jnp.zeros_like(slot_row_ref)
    slot_source_ref[...] = jnp.zeros_like(slot_source_ref)
    pivot_cols, moved_cols = [], []
    for k in range(STEPS):
        pivot = piv_ref[k : k + 1, :]
        owner = ((pivot >> 8) & 31).astype(F32)
        local = (((pivot >> 13) << 8) | (pivot & 255)).astype(F32)
        pivot = pivot.astype(F32)
        owner_col, local_col, pivot_col = column(owner), column(local), column(pivot)
        rank = pick((owner_col == owner) & (sub < lane), 1.0)
        rank_col = column(rank)
        position = lane_row + float(k * NB)
        moved = position
        source = (owner * PIECE + float(k * CAP) + rank).astype(jnp.int32)
        for earlier in range(k):
            same = pivot_cols[earlier] == position
            moved = jnp.where(pick(same, 1.0) > 0.0, pick(same, moved_cols[earlier]), moved)
            same = pivot_cols[earlier] == pivot
            source = jnp.where(
                pick(same, 1.0) > 0.0, top_index(pick(same, moved_cols[earlier])), source
            )
        moved_col = column(moved)
        pivot_cols.append(pivot_col)
        moved_cols.append(moved_col)
        source_ref[k : k + 1, :] = source
        mine = (owner_col == me) & (rank_col == lane_slot)
        filled = pick(mine, 1.0) > 0.0
        slot_row_ref[k : k + 1, :] = jnp.where(filled, pick(mine, local_col), float(WIDE)).astype(
            jnp.int32
        )
        slot_source_ref[k : k + 1, :] = top_index(jnp.where(filled, pick(mine, moved_col), 0.0))
        mine = (owner == me) & (rank == sub_slot)
        row = jnp.sum(jnp.where(mine, local, 0.0), axis=1, keepdims=True)
        packed_ref[k * CAP : (k + 1) * CAP, :] = jnp.dot(
            jnp.where(row == lane_wide, 1.0, 0.0),
            a_ref[...],
            precision=lax.Precision.HIGHEST,
            preferred_element_type=F32,
        )


def remote(src, dst, send_sem, recv_sem, target):
    return pltpu.make_async_remote_copy(
        src_ref=src,
        dst_ref=dst,
        send_sem=send_sem,
        recv_sem=recv_sem,
        device_id=target,
        device_id_type=pl.DeviceIdType.MESH,
    )


def place(x, y, core):
    return (lax.rem(x, SIDE) * SIDE + lax.rem(y, SIDE)) * 2 + core


GATHER_SEMS = 72


def plane_gather(view, rows, send_sem, recv_sem, sent):
    me = lax.axis_index("prow")
    core = lax.rem(me, 2)
    chip = me // 2
    cx, cy = chip // SIDE, lax.rem(chip, SIDE)
    half, part = rows // 2, rows // 4

    def at(h, i, j, c):
        return place(cx + i, cy + j, c) if h == 0 else place(cx + j, cy + i, c)

    def start(index, target, piece, row, count):
        copy = remote(
            view(piece, row, count),
            view(piece, row, count),
            send_sem.at[index],
            recv_sem.at[index],
            {"prow": target},
        )
        copy.start()
        sent.append(copy)

    def arrive(index, piece, row, count):
        remote(
            view(piece, row, count),
            view(piece, row, count),
            send_sem.at[index],
            recv_sem.at[index],
            {"prow": me},
        ).wait_recv()

    def first(h, n):
        return h * 4 + n

    def second(h, i, n):
        return 8 + (h * 4 + i) * 4 + n

    def across(h, i, j):
        return 40 + (h * 4 + i) * 4 + j

    def to_core(h, i, j):
        start(across(h, i, j), place(cx, cy, 1 - core), at(h, i, j, core), h * half, half)

    def start_second(h, i):
        piece = at(h, i, 0, core)
        start(second(h, i, 0), at(h, 0, 1, core), piece, h * half, half)
        start(second(h, i, 1), at(h, 0, 3, core), piece, h * half, half)

    for h in (0, 1):
        start(first(h, 0), at(h, 1, 0, core), me, h * half, half)
        start(first(h, 1), at(h, 3, 0, core), me, h * half, half)
    for h in (0, 1):
        start_second(h, 0)
        to_core(h, 0, 0)
    yield
    for n, i, on in ((0, 3, 1), (1, 1, 3)):
        for h in (0, 1):
            piece = at(h, i, 0, core)
            arrive(first(h, n), piece, h * half, half)
            start(first(h, 2 + n), at(h, on, 0, core), piece, h * half + n * part, part)
            start_second(h, i)
            to_core(h, i, 0)
            yield
    for h in (0, 1):
        for n in (0, 1):
            arrive(first(h, 2 + n), at(h, 2, 0, core), h * half + n * part, part)
        start_second(h, 2)
        to_core(h, 2, 0)
        yield
    for i in (0, 3, 1, 2):
        for n, j, on in ((0, 3, 1), (1, 1, 3)):
            for h in (0, 1):
                piece = at(h, i, j, core)
                arrive(second(h, i, n), piece, h * half, half)
                start(second(h, i, 2 + n), at(h, 0, on, core), piece, h * half + n * part, part)
                to_core(h, i, j)
                yield
    for i in (0, 3, 1, 2):
        for h in (0, 1):
            for n in (0, 1):
                arrive(second(h, i, 2 + n), at(h, i, 2, core), h * half + n * part, part)
            to_core(h, i, 2)
            yield
    for j in (0, 3, 1, 2):
        for i in (0, 3, 1, 2):
            for h in (0, 1):
                arrive(across(h, i, j), at(h, i, j, 1 - core), h * half, half)


class RingSpread:
    def __init__(self, view, per_source, send_sem, recv_sem):
        self.view, self.count = view, per_source
        self.send_sem, self.recv_sem = send_sem, recv_sem
        z = lax.axis_index("pcol")
        self.z = z
        self.lows = [self.range_in(0, z), self.range_in(1, z)]
        up = self.range_in(0, z + 1)
        down_low, down_high = self.range_in(1, lax.rem(z + RING - 1, RING))
        last = z == RING - 1
        self.outs = [
            (jnp.where(last, 0, up[0]), jnp.where(last, 0, up[1])),
            (down_low, down_high),
        ]
        self.to = [{"pcol": lax.rem(z + 1, RING)}, {"pcol": lax.rem(z + RING - 1, RING)}]
        inner = z < STEPS
        self.lag = [
            jnp.where(inner, 3, (z - 3) * 5 // 2),
            jnp.where(inner, 3, (RING - z) * 5 // 2),
        ]
        self.steps = max(3 * per_source + 3, 2 * per_source + 20)

    def meet(self, z):
        c = self.count
        return jnp.clip(2 * c + ((19 - 2 * z) * 5) // 4, 0, 4 * c)

    def range_in(self, way, z):
        c = self.count
        far = z >= STEPS
        if way == 0:
            return jnp.where(far, 0, (4 - z) * c), jnp.where(far, self.meet(z), 4 * c)
        return jnp.where(far, self.meet(z), 0), jnp.where(far, 4 * c, (3 - z) * c)

    def copy(self, way, g):
        return remote(
            self.view(g),
            self.view(g),
            self.send_sem.at[way, g],
            self.recv_sem.at[way, g],
            self.to[way],
        )

    def pass_on(self, way, g):
        low, high = self.outs[way]

        @pl.when((g >= low) & (g < high))
        def _():
            self.copy(way, g).start()

    def start(self):
        c = self.count

        @pl.when(self.z < STEPS)
        def _():
            @pl.loop(0, c)
            def _(i):
                self.pass_on(0, (3 - self.z) * c + i)
                self.pass_on(1, (4 - self.z) * c - 1 - i)

    def run(self, begin, end):
        if end <= begin:
            return

        @pl.loop(begin, end)
        def _(t):
            for way in (0, 1):
                low, high = self.lows[way]
                i = t - self.lag[way]

                @pl.when((i >= 0) & (i < high - low))
                def _():
                    g = low + i if way == 0 else high - 1 - i
                    self.copy(way, g).wait_recv()
                    self.pass_on(way, g)

    def finish(self):
        for way in (0, 1):
            low, high = self.outs[way]

            @pl.loop(low, high)
            def _(g):
                self.copy(way, g).wait_send()


def neighbours():
    me, z = lax.axis_index("prow"), lax.axis_index("pcol")
    core, chip = lax.rem(me, 2), me // 2
    cx, cy = chip // SIDE, lax.rem(chip, SIDE)
    return [
        {"prow": place(cx + 1, cy, core)},
        {"prow": place(cx + 3, cy, core)},
        {"prow": place(cx, cy + 1, core)},
        {"prow": place(cx, cy + 3, core)},
        {"prow": place(cx, cy, 1 - core)},
        {"pcol": lax.rem(z + 1, RING)},
        {"pcol": lax.rem(z + RING - 1, RING)},
    ]


def greet(targets):
    barrier = pltpu.get_barrier_semaphore()
    for target in targets:
        pl.semaphore_signal(
            barrier, inc=1, device_id=target, device_id_type=pl.DeviceIdType.MESH
        )
    return barrier


CHUNK = 32


def raw_kernel(
    source_ref, slot_source_ref, a_ref, packed_ref,
    cand_ref, panels_ref, piece_ref, moved_ref,
    slot_send, slot_recv, top_send, top_recv, deal_send, deal_recv, ring_send, ring_recv,
):
    me, z = lax.axis_index("prow"), lax.axis_index("pcol")
    barrier = greet(neighbours())
    for p in range(STEPS):

        @pl.when(me != p)
        def _():
            pl.semaphore_signal(
                barrier, inc=1, device_id={"prow": p}, device_id_type=pl.DeviceIdType.MESH
            )

    own = pl.multiple_of(me * PIECE, 8)
    cand_ref[pl.ds(own, SLOTS), :] = packed_ref[...]
    for p in range(STEPS):

        @pl.when(me == p)
        def _():
            cand_ref[pl.ds(own + SLOTS + 8 * p, 8), :] = a_ref[8 * p : 8 * p + 8, :]

        @pl.when(z == p)
        def _():
            panels_ref[p] = a_ref[:, 0:NB]

    pl.semaphore_wait(barrier, jnp.where(me < STEPS, 7 + PROWS - 1, 7))

    def deal(p, target):
        rows = pl.ds(pl.multiple_of(target * PIECE + SLOTS + 8 * p, 8), 8)
        return remote(
            a_ref.at[pl.ds(pl.multiple_of(target * 8, 8), 8), :],
            cand_ref.at[rows, :],
            deal_send.at[target],
            deal_recv.at[p],
            {"prow": target},
        )

    @pl.when(me < STEPS)
    def _():
        @pl.loop(1, PROWS)
        def _(i):
            deal(me, lax.rem(me + i, PROWS)).start()

    def chunk(g):
        per = WIDE // CHUNK
        return panels_ref.at[
            3 - g // per, pl.ds(pl.multiple_of(lax.rem(g, per) * CHUNK, CHUNK), CHUNK), :
        ]

    ring = RingSpread(chunk, WIDE // CHUNK, ring_send, ring_recv)

    def slot_view(piece, row, count):
        return cand_ref.at[pl.ds(pl.multiple_of(piece * PIECE + row, 8), count), :]

    def top_view(piece, row, count):
        return cand_ref.at[pl.ds(pl.multiple_of(piece * PIECE + SLOTS + row, 8), count), :]

    sent = []
    ring.start()
    done = 0
    for _ in plane_gather(slot_view, SLOTS, slot_send, slot_recv, sent):
        ring.run(done, done + 1)
        done += 1
    for p in range(STEPS):

        @pl.when(me != p)
        def _():
            deal(p, me).wait_recv()

    for n, _ in enumerate(plane_gather(top_view, TOPS, top_send, top_recv, sent)):
        if n % 2 == 0:
            ring.run(done, done + 1)
            done += 1

    def row_of(index):
        return cand_ref[pl.ds(index, 1), :]

    @pl.loop(0, 32)
    def _(i):
        piece_ref[pl.ds(i, 1), :] = row_of(
            source_ref[me // 8, lax.rem(me, 8) * 32 + i]
        )[:, 0:NB]

    @pl.loop(0, CAP)
    def _(i):
        for k in range(STEPS):
            moved_ref[pl.ds(k * CAP + i, 1), :] = row_of(slot_source_ref[k, i])

    ring.run(done, ring.steps)
    for copy in sent:
        copy.wait_send()
    ring.finish()

    @pl.when(me < STEPS)
    def _():
        @pl.loop(1, PROWS)
        def _(i):
            deal(me, lax.rem(me + i, PROWS)).wait_send()


def top_kernel(
    piece_ref, moved_ref, corner_ref, moved_panels_ref,
    plane_send, plane_recv, first_send, first_recv, ring_send, ring_recv,
):
    me, z = lax.axis_index("prow"), lax.axis_index("pcol")
    barrier = greet(neighbours())
    own = pl.multiple_of(me * 128, 128)
    for p in range(STEPS):

        @pl.when(z == p)
        def _():
            corner_ref[pl.ds(own + 32 * p, 32), :] = piece_ref[...]
            moved_panels_ref[p] = moved_ref[:, 0:NB]

    pl.semaphore_wait(barrier, 7)

    def first_view(g):
        return corner_ref.at[pl.ds(pl.multiple_of(own + (3 - g) * 32, 32), 32), :]

    def moved_view(g):
        per = SLOTS // CHUNK
        return moved_panels_ref.at[
            3 - g // per, pl.ds(pl.multiple_of(lax.rem(g, per) * CHUNK, CHUNK), CHUNK), :
        ]

    def corner_view(piece, row, count):
        return corner_ref.at[pl.ds(pl.multiple_of(piece * 128 + row, 32), count), :]

    first = RingSpread(first_view, 1, first_send, first_recv)
    ring = RingSpread(moved_view, SLOTS // CHUNK, ring_send, ring_recv)
    first.start()
    first.run(0, 45)
    ring.start()
    sent = []
    done = 0
    for _ in plane_gather(corner_view, 128, plane_send, plane_recv, sent):
        ring.run(done, done + 1)
        done += 1
    ring.run(done, 45)
    for copy in sent:
        copy.wait_send()
    first.finish()
    ring.finish()


def split(value):
    high = value.astype(jnp.bfloat16)
    return high, (value - high.astype(F32)).astype(jnp.bfloat16)


def dot(left, right):
    return jnp.dot(left, right, preferred_element_type=F32)


def eliminate_kernel(
    coord, source_ref, slot_row_ref, slot_source_ref, a_ref, cand_ref, panels_ref,
    corner_ref, moved_panels_ref, inv_ref, out_ref, work, high_ref, low_ref, keep,
):
    me, z = coord[0], coord[1]
    here = PAN
    for piece in range(PROWS):
        for q in range(STEPS):
            work[piece * 32 : piece * 32 + 32, q * NB : (q + 1) * NB] = corner_ref[
                piece * 128 + q * 32 : piece * 128 + q * 32 + 32, :
            ]
    for q in range(STEPS):
        work[here : here + WIDE, q * NB : (q + 1) * NB] = panels_ref[q]
    work[here : here + WIDE, PAN:] = a_ref[...]
    for k in range(STEPS):

        @pl.loop(0, NB, unroll=8)
        def _(j):
            work[pl.ds(k * NB + j, 1), PAN:] = cand_ref[pl.ds(source_ref[k, j], 1), :]

    for k in range(STEPS):

        @pl.loop(0, CAP)
        def _(s):
            row = pl.ds(here + slot_row_ref[k, s], 1)
            work[row, PAN:] = cand_ref[pl.ds(slot_source_ref[k, s], 1), :]
            for q in range(STEPS):
                work[row, q * NB : (q + 1) * NB] = moved_panels_ref[
                    q, pl.ds(k * CAP + s, 1), :
                ]

    row_i = lax.broadcasted_iota(jnp.int32, (NB, NB), 0)
    col_i = lax.broadcasted_iota(jnp.int32, (NB, NB), 1)
    total = PAN + WIDE
    for k in range(STEPS):
        top, begin = k * NB, (k + 1) * NB
        inverse = inv_ref[k].astype(F32)
        upper = jnp.where(row_i <= col_i, inverse, 0.0).astype(jnp.bfloat16)
        lower = jnp.where(
            row_i > col_i, inverse, jnp.where(row_i == col_i, 1.0, 0.0)
        ).astype(jnp.bfloat16)

        @pl.when(me == k)
        def _():
            keep[...] = work[top : top + NB, PAN : PAN + NB]

        for c in range(begin, total, NB):
            high, low = split(work[top : top + NB, c : c + NB])
            solved = dot(lower, high) + dot(lower, low)
            work[top : top + NB, c : c + NB] = solved
            high_ref[:, c : c + NB], low_ref[:, c : c + NB] = split(solved)

        @pl.loop(begin // NB, total // NB)
        def _(r):
            rows = pl.ds(pl.multiple_of(r * NB, NB), NB)
            high, low = split(work[rows, top : top + NB])
            factor = dot(high, upper) + dot(low, upper)
            work[rows, top : top + NB] = factor
            high, low = split(factor)
            for c in range(begin, total, NB):
                work[rows, c : c + NB] -= (
                    dot(high, high_ref[:, c : c + NB])
                    + dot(high, low_ref[:, c : c + NB])
                    + dot(low, high_ref[:, c : c + NB])
                )

    out_ref[...] = work[here : here + WIDE, PAN:]
    for q in range(STEPS):

        @pl.when(z == q)
        def _():
            out_ref[:, 0:NB] = work[here : here + WIDE, q * NB : (q + 1) * NB]

    for p in range(STEPS):

        @pl.when(me == p)
        def _():
            out_ref[0:NB, :] = work[p * NB : (p + 1) * NB, PAN:]
            for q in range(p):

                @pl.when(z == q)
                def _():
                    out_ref[0:NB, 0:NB] = work[p * NB : (p + 1) * NB, q * NB : (q + 1) * NB]

            @pl.when(z == p)
            def _():
                out_ref[0:NB, 0:NB] = keep[...]


VMEM = pl.BlockSpec(memory_space=pltpu.VMEM)
SMEM = pl.BlockSpec(memory_space=pltpu.SMEM)


def shape(*dims, dtype=F32):
    return jax.ShapeDtypeStruct(dims, dtype)


def prepare(coord, pivots, matrix):
    return pl.pallas_call(
        prep_kernel,
        out_shape=[
            shape(SLOTS, WIDE),
            shape(8, NB, dtype=jnp.int32),
            shape(8, 128, dtype=jnp.int32),
            shape(8, 128, dtype=jnp.int32),
        ],
        in_specs=[SMEM, VMEM, VMEM],
        out_specs=[VMEM] * 4,
        compiler_params=pltpu.CompilerParams(vmem_limit_bytes=16 * MIB),
    )(coord, pivots, matrix)


def gather_raw(source, slot_source, matrix, packed):
    chunks = STEPS * WIDE // CHUNK
    dma = pltpu.SemaphoreType.DMA
    return pl.pallas_call(
        raw_kernel,
        out_shape=[
            shape(PROWS * PIECE, WIDE),
            shape(STEPS, WIDE, NB),
            shape(32, NB),
            shape(SLOTS, WIDE),
        ],
        in_specs=[SMEM, SMEM, VMEM, VMEM],
        out_specs=[VMEM] * 4,
        scratch_shapes=[
            dma((GATHER_SEMS,)), dma((GATHER_SEMS,)),
            dma((GATHER_SEMS,)), dma((GATHER_SEMS,)),
            dma((PROWS,)), dma((STEPS,)),
            dma((2, chunks)), dma((2, chunks)),
        ],
        compiler_params=pltpu.CompilerParams(
            vmem_limit_bytes=32 * MIB, collective_id=0, has_side_effects=True
        ),
    )(source, slot_source, matrix, packed)


def gather_top(piece, moved):
    chunks = STEPS * SLOTS // CHUNK
    dma = pltpu.SemaphoreType.DMA
    return pl.pallas_call(
        top_kernel,
        out_shape=[shape(PROWS * 128, NB), shape(STEPS, SLOTS, NB)],
        in_specs=[VMEM] * 2,
        out_specs=[VMEM] * 2,
        scratch_shapes=[
            dma((GATHER_SEMS,)), dma((GATHER_SEMS,)),
            dma((2, STEPS)), dma((2, STEPS)),
            dma((2, chunks)), dma((2, chunks)),
        ],
        compiler_params=pltpu.CompilerParams(
            vmem_limit_bytes=32 * MIB, collective_id=1, has_side_effects=True
        ),
    )(piece, moved)


def eliminate(coord, source, slot_row, slot_source, matrix, cand, panels, corner, moved, inverses):
    return pl.pallas_call(
        eliminate_kernel,
        out_shape=shape(WIDE, WIDE),
        in_specs=[SMEM] * 4 + [VMEM] * 6,
        out_specs=VMEM,
        scratch_shapes=[
            pltpu.VMEM((PAN + WIDE + 8, PAN + WIDE), F32),
            pltpu.VMEM((NB, PAN + WIDE), jnp.bfloat16),
            pltpu.VMEM((NB, PAN + WIDE), jnp.bfloat16),
            pltpu.VMEM((NB, NB), F32),
        ],
        compiler_params=pltpu.CompilerParams(vmem_limit_bytes=48 * MIB),
    )(coord, source, slot_row, slot_source, matrix, cand, panels, corner, moved, inverses)


def per_device(matrix, pivots, block_inverses):
    coord = jnp.stack([lax.axis_index("prow"), lax.axis_index("pcol")]).astype(jnp.int32)
    packed, source, slot_row, slot_source = prepare(coord, pivots, matrix)
    cand, panels, piece, moved = gather_raw(source, slot_source, matrix, packed)
    corner, moved_panels = gather_top(piece, moved)
    return eliminate(
        coord, source, slot_row, slot_source, matrix, cand, panels, corner, moved_panels,
        block_inverses,
    )


def solution(mesh):
    placed = (P("prow", "pcol"), P(), P())
    return jax.shard_map(
        per_device, mesh=mesh, in_specs=placed, out_specs=P("prow", "pcol"), check_vma=False
    )
```

time: 1380 us -> 174 us (0.13)
  the two profiles are of different devices: /device:TPU:6 before, /device:TPU:257 now
where the time goes in v1:
time: 174 us
  Pallas kernels  164 us (94%)
  local copies, waits for them, and re-layouts  10.1 us (6%)
    pallas_call x1, Pallas kernels, gather_raw(): pl.pallas_call(raw_kernel, out_shape=[shape(PROWS * PIECE, WIDE), shape(S...  84.3 us
    pallas_call x1, Pallas kernels, gather_top(): pl.pallas_call(top_kernel, out_shape=[shape(PROWS * 128, NB), shape(STEPS...  51.1 us
    pallas_call x1, Pallas kernels, eliminate(): pl.pallas_call(eliminate_kernel, out_shape=shape(WIDE, WIDE), in_specs=[S...  24.6 us
    unnamed x14, local copies, waits for them, and re-layouts  10.1 us
    pallas_call x1, Pallas kernels, prepare(): pl.pallas_call(prep_kernel, out_shape=[shape(SLOTS, WIDE), shape(8, NB, d...  3.57 us

profile of v1, /device:TPU:257, one launch (start us, length us, event | category | flops | bytes accessed | tf_op | source)
XLA Modules:
  0.0 173.8 jit_solution(4393358168793798497)
XLA Ops:
  0.0 0.1 pad_add_fusion.coord
  0.1 0.0 copy-start
  0.1 1.2 copy-done
  1.3 0.0 copy-start.6
  1.3 0.7 copy-done.6
  2.0 3.6 %shard_map.37 = (f32[64,512]{1,0:T(8,128)S(1)}, s32[8,256]{1,0:T(8,128)S(1)}, s32[8,128]{1,0:T(8,128)S(1)}, s32[8,128]{1,0:T(8,128)S(1)}) custom-call(s32[2]{0:T(128)S(1)} %pad_add_fusion.coord, s32[4,256]{1,0:T(4,128)S(1)} %copy-done.6, f32[512,512]{1,0:T(8,128)S(1)} %copy-done), custom_call_target="tpu_custom_call" | custom-call | tf_op jit(solution)/shard_map/pallas_call | solution.py:555
  5.6 0.0 copy-start.1
  5.6 1.2 copy-done.1
  6.8 84.3 %shard_map.38 = (f32[3072,512]{1,0:T(8,128)S(1)}, f32[4,512,256]{2,1,0:T(8,128)S(1)}, f32[32,256]{1,0:T(8,128)S(1)}, f32[64,512]{1,0:T(8,128)S(1)}) custom-call(s32[8,256]{1,0:T(8,128)S(1)} %get-tuple-element.15.source_ref, s32[8,128]{1,0:T(8,128)S(1)} %get-tuple-element.17.slot_source_ref, f32[512,512]{1,0:T(8,128)S(1)} %copy-done.1, ...), custom_call_target="tpu_custom_call" | custom-call | tf_op jit(solution)/shard_map/pallas_call | solution.py:572
  91.1 0.0 copy-start.3
  91.2 2.7 %copy-done.3 = f32[3072,512]{1,0:T(8,128)} copy-done((f32[3072,512]{1,0:T(8,128)}, f32[3072,512]{1,0:T(8,128)S(1)}, u32[]{:S(2)}) %copy-start.3) | copy-done | bytes 6291480
  93.8 51.1 %shard_map.39 = (f32[4096,256]{1,0:T(8,128)S(1)}, f32[4,64,256]{2,1,0:T(8,128)S(1)}) custom-call(f32[32,256]{1,0:T(8,128)S(1)} %get-tuple-element.21.piece_ref, f32[64,512]{1,0:T(8,128)S(1)} %get-tuple-element.22.moved_ref), custom_call_target="tpu_custom_call" | custom-call | tf_op jit(solution)/shard_map/pallas_call | solution.py:597
  144.9 0.0 copy-start.4
  144.9 2.0 %copy-done.4 = f32[4096,256]{1,0:T(8,128)} copy-done((f32[4096,256]{1,0:T(8,128)}, f32[4096,256]{1,0:T(8,128)S(1)}, u32[]{:S(2)}) %copy-start.4) | copy-done | bytes 4194328
  146.9 0.0 copy-start.2
  146.9 1.2 copy-done.2
  148.1 0.0 copy-start.5
  148.1 1.0 copy-done.5
  149.2 24.6 %shard_map.40 = f32[512,512]{1,0:T(8,128)} custom-call(s32[2]{0:T(128)S(1)} %pad_add_fusion.coord, s32[8,256]{1,0:T(8,128)S(1)} %get-tuple-element.15.source_ref, s32[8,128]{1,0:T(8,128)S(1)} %get-tuple-element.16.slot_row_ref, s32[8,128]{1,0:T(8,128)S(1)} %get-tuple-element.17.slot_source_ref, f32[512,512]{1,0:T(8,128)S(1)} %copy-done.2, ...), custom_call_target="tpu_custom_call" | custom-call | tf_op jit(solution)/shard_map/pallas_call | solution.py:614
Async XLA Ops:
  0.1 1.2 copy-start
  1.3 0.7 copy-start.6
  5.6 1.2 copy-start.1
  91.1 2.7 %copy-start.3 = (f32[3072,512]{1,0:T(8,128)}, f32[3072,512]{1,0:T(8,128)S(1)}, u32[]{:S(2)}) copy-start(f32[3072,512]{1,0:T(8,128)S(1)} %get-tuple-element.19.cand_ref) | copy-start | bytes 18874372
  144.9 2.0 %copy-start.4 = (f32[4096,256]{1,0:T(8,128)}, f32[4096,256]{1,0:T(8,128)S(1)}, u32[]{:S(2)}) copy-start(f32[4096,256]{1,0:T(8,128)S(1)} %get-tuple-element.23.corner_ref) | copy-start | bytes 12582916
  146.9 1.2 copy-start.2
  148.1 1.0 copy-start.5

commit v2 on v0

v2 whole, which is shorter than its diff:
```python
import jax
import jax.numpy as jnp
from jax import lax
from jax.experimental import pallas as pl
from jax.experimental.pallas import tpu as pltpu
from jax.sharding import PartitionSpec as P

NB = 256
STEPS = 4
CAP = 16
SLOTS = STEPS * CAP
TOPS = 32
PIECE = SLOTS + TOPS
DEAL = 32
WINDOW = 3
SIDE = 4
PROWS = 32
RING = 16
WIDE = 512
PAN = STEPS * NB
CHUNK = 32
LATE = 32
F32 = jnp.float32
BF16 = jnp.bfloat16
MIB = 1024 * 1024


def prep_kernel(coord, piv_ref, source_ref, slot_ref, local_ref, lanes_ref):
    me = coord[0].astype(F32)
    sub = lax.broadcasted_iota(jnp.int32, (NB, NB), 0)
    lane = lax.broadcasted_iota(jnp.int32, (NB, NB), 1)
    lane_row = lax.broadcasted_iota(jnp.int32, (1, NB), 1).astype(F32)
    lane_slot = lax.broadcasted_iota(jnp.int32, (NB, 128), 1).astype(F32)

    def column(row):
        return jnp.sum(jnp.where(sub == lane, row, 0.0), axis=1, keepdims=True)

    def pick(mask, value):
        return jnp.sum(jnp.where(mask, value, 0.0), axis=0, keepdims=True)

    def top_index(row):
        t = row.astype(jnp.int32)
        return piece_index((t & 255) >> 3) + SLOTS + (t >> 8) * 8 + (t & 7)

    def piece_index(p):
        return ((p & 1) * 16 + (p >> 1)) << 7

    source_ref[...] = jnp.zeros_like(source_ref)
    slot_ref[...] = jnp.zeros_like(slot_ref)
    filled = jnp.zeros((1, 128), F32)
    slot_row = jnp.zeros((1, 128), F32)
    slot_top = jnp.zeros((1, 128), F32)
    pivot_cols, moved_cols = [], []
    for k in range(STEPS):
        pivot = piv_ref[k : k + 1, :]
        owner = ((pivot >> 8) & 31).astype(F32)
        local = (((pivot >> 13) << 8) | (pivot & 255)).astype(F32)
        pivot = pivot.astype(F32)
        owner_col, local_col, pivot_col = column(owner), column(local), column(pivot)
        rank = pick((owner_col == owner) & (sub < lane), 1.0) + float(k * CAP)
        rank_col = column(rank)
        position = lane_row + float(k * NB)
        moved = position
        source = piece_index(owner.astype(jnp.int32)) + rank.astype(jnp.int32)
        mine = jnp.where(owner == me, local, -1.0)
        for earlier in range(k):
            same = pivot_cols[earlier] == position
            moved = jnp.where(pick(same, 1.0) > 0.0, pick(same, moved_cols[earlier]), moved)
            same = pivot_cols[earlier] == pivot
            hit = pick(same, 1.0) > 0.0
            top = pick(same, moved_cols[earlier])
            source = jnp.where(hit, top_index(top), source)
            block = (top.astype(jnp.int32) >> 8).astype(F32)
            mine = jnp.where(hit, jnp.where(block == me, top - block * NB, -1.0), mine)
        moved_col = column(moved)
        pivot_cols.append(pivot_col)
        moved_cols.append(moved_col)
        source_ref[k : k + 1, :] = source
        local_ref[k * NB : (k + 1) * NB, :] = column(mine)
        here = (owner_col == me) & (rank_col == lane_slot)
        filled += pick(here, 1.0)
        slot_row += pick(here, local_col)
        slot_top += pick(here, moved_col)
    slot_ref[0:1, :] = slot_row.astype(jnp.int32)
    slot_ref[1:2, :] = top_index(slot_top) - SLOTS
    lanes_ref[...] = jnp.broadcast_to(jnp.where(filled > 0.0, slot_row, -1.0), (8, 128))


def remote(src, dst, send_sem, recv_sem, target):
    return pltpu.make_async_remote_copy(
        src_ref=src,
        dst_ref=dst,
        send_sem=send_sem,
        recv_sem=recv_sem,
        device_id=target,
        device_id_type=pl.DeviceIdType.MESH,
    )


def place(x, y, core):
    return (lax.rem(x, SIDE) * SIDE + lax.rem(y, SIDE)) * 2 + core


GATHER_SEMS = 20


class PlaneGather:
    def __init__(self, buffer, first, rows, send_sem, recv_sem, sent):
        me = lax.axis_index("prow")
        self.buffer, self.sent = buffer, sent
        self.send_sem, self.recv_sem = send_sem, recv_sem
        self.core, chip = lax.rem(me, 2), me // 2
        self.cx, self.cy = chip // SIDE, lax.rem(chip, SIDE)
        self.me = me
        self.rows = [pl.ds(first, rows // 2), pl.ds(first + rows // 2, rows // 2)]
        self.events = [
            self.start,
            lambda: self.turn(0),
            lambda: self.turn(1),
            *[lambda h=h, d=d: self.land(h, d) for d in (1, 3, 2) for h in (0, 1)],
            self.end,
        ]
        self.at_event = 0

    def one(self, h, d):
        if h == 0:
            x, y = lax.rem(self.cx + d, SIDE), self.cy
        else:
            x, y = self.cx, lax.rem(self.cy + d, SIDE)
        return self.buffer.at[self.core * SIDE + x, y, self.rows[h]]

    def line(self, h, d, core):
        if h == 0:
            y = lax.rem(self.cy + d, SIDE)
            return self.buffer.at[pl.ds(core * SIDE, SIDE), y, self.rows[h]]
        x = lax.rem(self.cx + d, SIDE)
        return self.buffer.at[core * SIDE + x, :, self.rows[h]]

    def device(self, h, d):
        x, y = (self.cx + d, self.cy) if h == 0 else (self.cx, self.cy + d)
        return place(x, y, self.core)

    def copy(self, index, part, target):
        return remote(
            part, part, self.send_sem.at[index], self.recv_sem.at[index], {"prow": target}
        )

    def send(self, index, part, target):
        copy = self.copy(index, part, target)
        copy.start()
        self.sent.append(copy)

    def arrive(self, index, part):
        self.copy(index, part, self.me).wait_recv()

    def across(self, h, d):
        other = place(self.cx, self.cy, 1 - self.core)
        self.send(12 + h * 4 + d, self.line(h, d, self.core), other)

    def start(self):
        for d in (1, 3, 2):
            for h in (0, 1):
                self.send(h * 3 + d - 1, self.one(h, 0), self.device(h, d))

    def turn(self, h):
        for d in (1, 3, 2):
            self.arrive(h * 3 + d - 1, self.one(h, SIDE - d))
        for d in (1, 3, 2):
            self.send(6 + h * 3 + d - 1, self.line(h, 0, self.core), self.device(1 - h, d))
        self.across(h, 0)

    def land(self, h, d):
        self.arrive(6 + h * 3 + d - 1, self.line(h, SIDE - d, self.core))
        self.across(h, SIDE - d)

    def end(self):
        for h in (0, 1):
            for d in (0, 3, 1, 2):
                self.arrive(12 + h * 4 + d, self.line(h, d, 1 - self.core))

    def step(self):
        if self.at_event < len(self.events):
            self.events[self.at_event]()
            self.at_event += 1

    def drain(self):
        while self.at_event < len(self.events):
            self.step()


class RingSpread:
    def __init__(self, view, total, above, own, lag, skew, send_sem, recv_sem):
        self.view, self.total, self.skew = view, total, skew
        self.send_sem, self.recv_sem = send_sem, recv_sem
        z = lax.axis_index("pcol")
        inner = z < STEPS
        self.own = jnp.where(inner, own, 0)
        self.seq = [
            (jnp.where(inner, above, 0), jnp.where(inner, total, self.meet(z))),
            (jnp.where(inner, 0, self.meet(z)), jnp.where(inner, above + own, total)),
        ]
        before = lax.rem(z + RING - 1, RING)
        self.outs = [
            (
                self.seq[0][0],
                jnp.where(
                    z == RING - 1,
                    self.seq[0][0],
                    jnp.where(z < STEPS - 1, total, self.meet(z + 1)),
                ),
            ),
            (
                jnp.where(
                    z == STEPS, self.seq[1][1], jnp.where(before >= STEPS, self.meet(before), 0)
                ),
                self.seq[1][1],
            ),
        ]
        self.to = [{"pcol": lax.rem(z + 1, RING)}, {"pcol": before}]
        self.lag = [
            jnp.where(inner, 0, (z - 3) * lag),
            jnp.where(inner, 0, (RING - z) * lag),
        ]
        self.done = 0
        self.steps = total
        for c in range(STEPS, RING):
            met = min(max((2 * total + (19 - 2 * c) * skew) // 4, 0), total)
            self.steps = max(
                self.steps, (c - 3) * lag + met, (RING - c) * lag + total - met
            )

    def meet(self, z):
        return jnp.clip((2 * self.total + (19 - 2 * z) * self.skew) // 4, 0, self.total)

    def copy(self, way, g):
        return remote(
            self.view(g),
            self.view(g),
            self.send_sem.at[way, g],
            self.recv_sem.at[way, g],
            self.to[way],
        )

    def pass_on(self, way, g):
        low, high = self.outs[way]

        @pl.when((g >= low) & (g < high))
        def _():
            earlier = g - WINDOW if way == 0 else g + WINDOW

            @pl.when((earlier >= low) & (earlier < high))
            def _():
                self.copy(way, earlier).wait_send()

            self.copy(way, g).start()

    def run(self, count):
        begin, end = self.done, min(self.done + count, self.steps)
        if end <= begin:
            return
        self.done = end

        @pl.loop(begin, end)
        def _(t):
            for way in (0, 1):
                low, high = self.seq[way]
                i = t - self.lag[way]

                @pl.when((i >= 0) & (i < high - low))
                def _():
                    g = low + i if way == 0 else high - 1 - i

                    @pl.when(i >= self.own)
                    def _():
                        self.copy(way, g).wait_recv()

                    self.pass_on(way, g)

    def finish(self):
        for way in (0, 1):
            low, high = self.outs[way]

            @pl.loop(0, WINDOW)
            def _(i):
                g = high - 1 - i if way == 0 else low + i

                @pl.when((g >= low) & (g < high))
                def _():
                    self.copy(way, g).wait_send()


def weave(*streams):
    order = sorted(
        ((i + 0.5) / count, n) for n, (_, count) in enumerate(streams) for i in range(count)
    )
    for _, n in order:
        streams[n][0]()


def signal(target):
    pl.semaphore_signal(
        pltpu.get_barrier_semaphore(),
        inc=1,
        device_id=target,
        device_id_type=pl.DeviceIdType.MESH,
    )


def split(value):
    high = value.astype(BF16)
    return high, (value - high.astype(F32)).astype(BF16)


def dot(left, right):
    return jnp.dot(left, right, preferred_element_type=F32)


def choose(onehot, value):
    high, rest = split(value)
    middle = (value - high.astype(F32)) - rest.astype(F32)
    return (dot(onehot, high) + dot(onehot, rest)) + dot(onehot, middle.astype(BF16))


def main_kernel(
    source_ref, slot_ref, a_ref, local_ref, lanes_ref, inv_ref,
    out_ref,
    cand_ref, tops_ref, panels_ref, corner_ref, moved_ref, moved_panels_ref, pack_ref, dealt_ref,
    work, high_ref, low_ref, keep,
    slot_send, slot_recv, top_send, top_recv, corner_send, corner_recv,
    share_send, share_recv, deal_send, deal_recv,
    raw_send, raw_recv, first_send, first_recv, late_send, late_recv,
):
    me, z = lax.axis_index("prow"), lax.axis_index("pcol")
    core, chip = lax.rem(me, 2), me // 2
    cx, cy = chip // SIDE, lax.rem(chip, SIDE)
    block = me // 8
    dealing = z < STEPS

    signal({"pcol": lax.rem(z + 1, RING)})
    signal({"pcol": lax.rem(z + RING - 1, RING)})

    @pl.when(dealing)
    def _():
        @pl.loop(1, PROWS)
        def _(i):
            signal({"prow": lax.rem(me + i, PROWS)})

    @pl.when(z >= STEPS)
    def _():
        signal({"prow": place(cx + 1, cy, core)})
        signal({"prow": place(cx + 3, cy, core)})
        signal({"prow": place(cx + 2, cy, core)})
        signal({"prow": place(cx, cy + 2, core)})
        signal({"prow": place(cx, cy + 1, core)})
        signal({"prow": place(cx, cy + 3, core)})
        signal({"prow": place(cx, cy, 1 - core)})
        for p in range(STEPS):

            @pl.when(me != p)
            def _():
                signal({"prow": p})

    side = core * SIDE + cx

    @pl.loop(0, SLOTS, unroll=8)
    def _(s):
        cand_ref[side, cy, pl.ds(s, 1), :] = a_ref[pl.ds(slot_ref[0, s], 1), :]

    for p in range(STEPS):

        @pl.when(me == p)
        def _():
            tops_ref[side, cy, 8 * p : 8 * p + 8, :] = a_ref[8 * p : 8 * p + 8, :]

        @pl.when(z == p)
        def _():
            panels_ref[p] = a_ref[:, 0:NB]

    @pl.when(dealing)
    def _():
        row_at = lax.broadcasted_iota(jnp.int32, (NB, WIDE), 1).astype(F32)

        @pl.loop(0, STEPS)
        def _(k):
            rows = pl.ds(pl.multiple_of(k * NB, NB), NB)
            onehot = jnp.where(local_ref[rows, :] == row_at, 1.0, 0.0).astype(BF16)
            pack_ref[rows, :] = choose(onehot, a_ref[:, 0:NB])

        dealt_ref[pl.ds(pl.multiple_of(me * DEAL, DEAL), DEAL), :] = pack_ref[
            pl.ds(pl.multiple_of(me * DEAL, DEAL), DEAL), :
        ]

    met = jnp.where(me < STEPS, 9 + PROWS - 1, 9)
    pl.semaphore_wait(pltpu.get_barrier_semaphore(), jnp.where(dealing, PROWS + 1, met))

    def share(p, target):
        rows = pl.ds(pl.multiple_of(8 * p, 8), 8)
        far = target // 2
        return remote(
            a_ref.at[pl.ds(pl.multiple_of(target * 8, 8), 8), :],
            tops_ref.at[lax.rem(target, 2) * SIDE + far // SIDE, lax.rem(far, SIDE), rows],
            share_send.at[target],
            share_recv.at[p],
            {"prow": target},
        )

    def deal(source, target):
        return remote(
            pack_ref.at[pl.ds(pl.multiple_of(target * DEAL, DEAL), DEAL), :],
            dealt_ref.at[pl.ds(pl.multiple_of(source * DEAL, DEAL), DEAL), :],
            deal_send.at[target],
            deal_recv.at[source],
            {"prow": target},
        )

    @pl.when(me < STEPS)
    def _():
        @pl.loop(1, PROWS)
        def _(i):
            share(me, lax.rem(me + i, PROWS)).start()

    @pl.when(dealing)
    def _():
        @pl.loop(1, PROWS)
        def _(i):
            target = lax.rem(me + i, PROWS)

            @pl.when(target // 8 != z)
            def _():
                deal(me, target).start()

    per = WIDE // CHUNK

    def raw_view(g):
        return panels_ref.at[
            3 - g // per, pl.ds(pl.multiple_of(lax.rem(g, per) * CHUNK, CHUNK), CHUNK), :
        ]

    def first_view(g):
        return corner_ref.at[side, cy, pl.ds(pl.multiple_of(g * 32, 32), 32)]

    late = SLOTS // LATE

    def late_view(g):
        return moved_panels_ref.at[
            3 - g // late, pl.ds(pl.multiple_of(lax.rem(g, late) * LATE, LATE), LATE), :
        ]

    raw = RingSpread(raw_view, STEPS * per, (3 - z) * per, per, 4, 8, raw_send, raw_recv)
    above = 3 - z - jnp.where(block > z, 1, 0)
    mine = jnp.where(block == z, 0, 1)
    first = RingSpread(first_view, 3, above, mine, 4, 8, first_send, first_recv)
    moved = RingSpread(
        late_view, STEPS * late, (3 - z) * late, late, 4, 8, late_send, late_recv
    )
    sent = []
    slots = PlaneGather(cand_ref, 0, SLOTS, slot_send, slot_recv, sent)
    tops = PlaneGather(tops_ref, 0, TOPS, top_send, top_recv, sent)
    corner = PlaneGather(corner_ref, 0, 96, corner_send, corner_recv, sent)

    def row_of(index):
        return cand_ref[index >> 9, (index >> 7) & 3, pl.ds(index & 127, 1), :]

    chosen = [0]

    def choose_rows():
        n = chosen[0]
        chosen[0] += 1

        @pl.loop(0, 32, unroll=8)
        def _(j):
            work[pl.ds(n * 32 + j, 1), PAN:] = row_of(source_ref[n // 8, n % 8 * 32 + j])

    def advance(*rings):
        return [(lambda ring=ring: ring.run(1), count) for ring, count in rings]

    slots.step()
    raw.run(PLAN[0])
    for p in range(STEPS):

        @pl.when(me != p)
        def _():
            share(p, me).wait_recv()

    tops.step()
    raw.run(PLAN[1])
    tops.step()
    tops.step()
    raw.run(PLAN[2])

    @pl.when(dealing & (block != z))
    def _():
        @pl.loop(1, PROWS)
        def _(i):
            deal(lax.rem(me + i, PROWS), me).wait_recv()

        total = dealt_ref[0:DEAL, :]
        for p in range(1, PROWS):
            total += dealt_ref[p * DEAL : (p + 1) * DEAL, :]
        corner_ref[side, cy, pl.ds(pl.multiple_of(above * 32, 32), 32), :] = total

    weave(*advance((first, PLAN[3]), (raw, PLAN[3])), (tops.step, 7))

    @pl.loop(0, SLOTS, unroll=8)
    def _(s):
        index = slot_ref[1, s]
        moved_ref[pl.ds(s, 1), :] = tops_ref[
            index >> 9, (index >> 7) & 3, pl.ds(index & 127, 1), :
        ]

    for p in range(STEPS):

        @pl.when(z == p)
        def _():
            moved_panels_ref[p] = moved_ref[:, 0:NB]

    slots.step()
    slots.step()
    left = first.steps - PLAN[3]
    weave(*advance((first, left), (raw, left), (moved, left)))
    corner.step()
    weave(*advance((moved, PLAN[4]), (raw, PLAN[4])))
    corner.step()
    corner.step()
    weave(*advance((moved, PLAN[5]), (raw, PLAN[5])), (slots.step, 7))
    moved.run(moved.steps)
    cand_ref[:, :, SLOTS:, :] = tops_ref[...]
    weave(*advance((raw, PLAN[6])), (corner.step, 7), (choose_rows, 32))


    slot_at = lanes_ref[0:1, :]
    row_at = lax.broadcasted_iota(jnp.int32, (WIDE, 128), 0).astype(F32)
    step_at = lax.broadcasted_iota(jnp.int32, (WIDE, 128), 1) // CAP
    match = jnp.where(row_at == slot_at, 1.0, 0.0)
    last = jnp.max(jnp.where(match > 0.0, step_at.astype(F32), -1.0), axis=1, keepdims=True)
    hit = last >= 0.0
    onehot = jnp.where((step_at.astype(F32) == last) & (match > 0.0), 1.0, 0.0)
    onehot = onehot.astype(BF16)[:, 0:SLOTS]
    for c in range(0, WIDE, NB):
        work[PAN:, PAN + c : PAN + c + NB] = jnp.where(
            hit, choose(onehot, moved_ref[:, c : c + NB]), a_ref[:, c : c + NB]
        )

    for k in range(STEPS):
        for q in range(STEPS):
            if q != k:
                g = 3 - q - (1 if k > q else 0)
                for i in range(8):
                    far = k * 4 + i // 2
                    work[k * NB + i * 32 : k * NB + i * 32 + 32, q * NB : (q + 1) * NB] = (
                        corner_ref[
                            i % 2 * SIDE + far // SIDE, far % SIDE, g * 32 : g * 32 + 32, :
                        ]
                    )
    row_i = lax.broadcasted_iota(jnp.int32, (NB, NB), 0)
    col_i = lax.broadcasted_iota(jnp.int32, (NB, NB), 1)
    total = PAN + WIDE

    def eliminate(k, rows):
        top, begin = k * NB, (k + 1) * NB
        upper = jnp.where(row_i <= col_i, inv_ref[k].astype(F32), 0.0).astype(BF16)
        high, low = split(work[rows, top : top + NB])
        factor = dot(high, upper) + dot(low, upper)
        work[rows, top : top + NB] = factor
        high, low = split(factor)
        for c in range(begin, total, NB):
            work[rows, c : c + NB] -= (
                dot(high, high_ref[top : top + NB, c : c + NB])
                + dot(high, low_ref[top : top + NB, c : c + NB])
                + dot(low, high_ref[top : top + NB, c : c + NB])
            )

    for k in range(STEPS):
        top, begin = k * NB, (k + 1) * NB
        lower = jnp.where(
            row_i > col_i, inv_ref[k].astype(F32), jnp.where(row_i == col_i, 1.0, 0.0)
        ).astype(BF16)

        @pl.when(me == k)
        def _():
            keep[...] = work[top : top + NB, PAN : PAN + NB]

        for c in range(begin, total, NB):
            high, low = split(work[top : top + NB, c : c + NB])
            solved = dot(lower, high) + dot(lower, low)
            work[top : top + NB, c : c + NB] = solved
            high, low = split(solved)
            high_ref[top : top + NB, c : c + NB] = high
            low_ref[top : top + NB, c : c + NB] = low
        raw.run(2)
        if begin < PAN:

            @pl.loop(k + 1, STEPS)
            def _(r):
                eliminate(k, pl.ds(pl.multiple_of(r * NB, NB), NB))

            raw.run(2)

    raw.run(raw.steps)
    for q in range(STEPS):
        work[PAN:, q * NB : (q + 1) * NB] = jnp.where(
            hit, choose(onehot, moved_panels_ref[q]), panels_ref[q]
        )

    @pl.loop(STEPS, total // NB)
    def _(r):
        for k in range(STEPS):
            eliminate(k, pl.ds(pl.multiple_of(r * NB, NB), NB))

    out_ref[...] = work[PAN:, PAN:]
    for q in range(STEPS):

        @pl.when(z == q)
        def _():
            out_ref[:, 0:NB] = work[PAN:, q * NB : (q + 1) * NB]

    for p in range(STEPS):

        @pl.when(me == p)
        def _():
            out_ref[0:NB, :] = work[p * NB : (p + 1) * NB, PAN:]
            for q in range(p):

                @pl.when(z == q)
                def _():
                    out_ref[0:NB, 0:NB] = work[p * NB : (p + 1) * NB, q * NB : (q + 1) * NB]

            @pl.when(z == p)
            def _():
                out_ref[0:NB, 0:NB] = keep[...]

    for copy in sent:
        copy.wait_send()
    for ring in (raw, first, moved):
        ring.finish()

    @pl.when(me < STEPS)
    def _():
        @pl.loop(1, PROWS)
        def _(i):
            share(me, lax.rem(me + i, PROWS)).wait_send()

    @pl.when(dealing)
    def _():
        @pl.loop(1, PROWS)
        def _(i):
            target = lax.rem(me + i, PROWS)

            @pl.when(target // 8 != z)
            def _():
                deal(me, target).wait_send()


PLAN = (12, 6, 10, 10, 5, 8, 8)
VMEM = pl.BlockSpec(memory_space=pltpu.VMEM)
SMEM = pl.BlockSpec(memory_space=pltpu.SMEM)


def shape(*dims, dtype=F32):
    return jax.ShapeDtypeStruct(dims, dtype)


def prepare(coord, pivots):
    return pl.pallas_call(
        prep_kernel,
        out_shape=[
            shape(8, NB, dtype=jnp.int32),
            shape(8, 128, dtype=jnp.int32),
            shape(PAN, 1),
            shape(8, 128),
        ],
        in_specs=[SMEM, VMEM],
        out_specs=[VMEM] * 4,
        compiler_params=pltpu.CompilerParams(vmem_limit_bytes=16 * MIB),
    )(coord, pivots)


def factor(source, slot, matrix, local, lanes, inverses):
    dma = pltpu.SemaphoreType.DMA
    raw, late = STEPS * WIDE // CHUNK, STEPS * SLOTS // LATE
    return pl.pallas_call(
        main_kernel,
        out_shape=shape(WIDE, WIDE),
        in_specs=[SMEM] * 2 + [VMEM] * 4,
        out_specs=VMEM,
        scratch_shapes=[
            pltpu.VMEM((2 * SIDE, SIDE, PIECE, WIDE), F32),
            pltpu.VMEM((2 * SIDE, SIDE, TOPS, WIDE), F32),
            pltpu.VMEM((STEPS, WIDE, NB), F32),
            pltpu.VMEM((2 * SIDE, SIDE, 96, NB), F32),
            pltpu.VMEM((SLOTS, WIDE), F32),
            pltpu.VMEM((STEPS, SLOTS, NB), F32),
            pltpu.VMEM((PAN, NB), F32),
            pltpu.VMEM((PAN, NB), F32),
            pltpu.VMEM((PAN + WIDE, PAN + WIDE), F32),
            pltpu.VMEM((PAN, PAN + WIDE), BF16),
            pltpu.VMEM((PAN, PAN + WIDE), BF16),
            pltpu.VMEM((NB, NB), F32),
            *[dma((GATHER_SEMS,))] * 6,
            dma((PROWS,)), dma((STEPS,)), dma((PROWS,)), dma((PROWS,)),
            dma((2, raw)), dma((2, raw)), dma((2, 3)), dma((2, 3)),
            dma((2, late)), dma((2, late)),
        ],
        compiler_params=pltpu.CompilerParams(
            vmem_limit_bytes=52 * MIB, collective_id=0, has_side_effects=True
        ),
    )(source, slot, matrix, local, lanes, inverses)


def per_device(matrix, pivots, block_inverses):
    coord = jnp.stack([lax.axis_index("prow"), lax.axis_index("pcol")]).astype(jnp.int32)
    source, slot, local, lanes = prepare(coord, pivots)
    return factor(source, slot, matrix, local, lanes, block_inverses)


def solution(mesh):
    placed = (P("prow", "pcol"), P(), P())
    return jax.shard_map(
        per_device, mesh=mesh, in_specs=placed, out_specs=P("prow", "pcol"), check_vma=False
    )
```

time: 1380 us -> 122 us (0.09)
  the two profiles are of different devices: /device:TPU:6 before, /device:TPU:321 now
where the time goes in v2:
time: 122 us
  Pallas kernels  118 us (97%)
  local copies, waits for them, and re-layouts  3.91 us (3%)
    pallas_call x1, Pallas kernels, factor(): pl.pallas_call(main_kernel, out_shape=shape(WIDE, WIDE), in_specs=[SMEM]...  116 us
    unnamed x5, local copies, waits for them, and re-layouts  3.91 us

profile of v2, /device:TPU:321, one launch (start us, length us, event | category | flops | bytes accessed | tf_op | source)
XLA Modules:
  0.0 121.8 jit_solution(4815094139758368363)
XLA Ops:
  0.0 0.0 copy-start.1
  0.0 0.1 pad_add_fusion.coord
  0.1 0.6 copy-done.1
  0.7 2.0 %shard_map.37 = (s32[8,256]{1,0:T(8,128)S(1)}, s32[8,128]{1,0:T(8,128)S(1)}, f32[1024,1]{1,0:T(8,128)S(1)}, f32[8,128]{1,0:T(8,128)S(1)}) custom-call(s32[2]{0:T(128)S(1)} %pad_add_fusion.coord, s32[4,256]{1,0:T(4,128)S(1)} %copy-done.1), custom_call_target="tpu_custom_call" | custom-call | tf_op jit(solution)/shard_map/pallas_call | solution.py:664
  2.7 0.0 copy-start
  2.7 1.0 copy-done
  3.7 115.8 %shard_map.38 = f32[512,512]{1,0:T(8,128)} custom-call(s32[8,256]{1,0:T(8,128)S(1)} %get-tuple-element.9.source_ref, s32[8,128]{1,0:T(8,128)S(1)} %get-tuple-element.10.slot_ref, f32[512,512]{1,0:T(8,128)} %a_ref.1, f32[1024,1]{1,0:T(8,128)S(1)} %get-tuple-element.11.local_ref, f32[8,128]{1,0:T(8,128)S(1)} %get-tuple-element.12.lanes_ref, ...), custom_call_target="tpu_custom_call" | custom-call | tf_op jit(solution)/shard_map/pallas_call | solution.py:681
  119.5 2.3 %copy.5 = f32[512,512]{1,0:T(8,128)} copy(f32[512,512]{1,0:T(8,128)} %shard_map.38) | data formatting | bytes 2097152
Async XLA Ops:
  0.0 0.7 copy-start.1
  2.7 1.0 copy-start

commit v3 on v2

--- a/solution.py
+++ b/solution.py
@@ -12,7 +12,7 @@
 TOPS = 32
 PIECE = SLOTS + TOPS
 DEAL = 32
-WINDOW = 3
+WINDOW = 4
 SIDE = 4
 PROWS = 32
 RING = 16
@@ -325,7 +325,7 @@
     source_ref, slot_ref, a_ref, local_ref, lanes_ref, inv_ref,
     out_ref,
     cand_ref, tops_ref, panels_ref, corner_ref, moved_ref, moved_panels_ref, pack_ref, dealt_ref,
-    work, high_ref, low_ref, keep,
+    work, parts_ref, keep,
     slot_send, slot_recv, top_send, top_recv, corner_send, corner_recv,
     share_send, share_recv, deal_send, deal_recv,
     raw_send, raw_recv, first_send, first_recv, late_send, late_recv,
@@ -449,9 +449,9 @@
     raw = RingSpread(raw_view, STEPS * per, (3 - z) * per, per, 4, 8, raw_send, raw_recv)
     above = 3 - z - jnp.where(block > z, 1, 0)
     mine = jnp.where(block == z, 0, 1)
-    first = RingSpread(first_view, 3, above, mine, 4, 8, first_send, first_recv)
+    first = RingSpread(first_view, 3, above, mine, 3, 8, first_send, first_recv)
     moved = RingSpread(
-        late_view, STEPS * late, (3 - z) * late, late, 4, 8, late_send, late_recv
+        late_view, STEPS * late, (3 - z) * late, late, 3, 8, late_send, late_recv
     )
     sent = []
     slots = PlaneGather(cand_ref, 0, SLOTS, slot_send, slot_recv, sent)
@@ -563,12 +563,9 @@
         factor = dot(high, upper) + dot(low, upper)
         work[rows, top : top + NB] = factor
         high, low = split(factor)
+        left = jnp.concatenate([high, high, low], axis=1)
         for c in range(begin, total, NB):
-            work[rows, c : c + NB] -= (
-                dot(high, high_ref[top : top + NB, c : c + NB])
-                + dot(high, low_ref[top : top + NB, c : c + NB])
-                + dot(low, high_ref[top : top + NB, c : c + NB])
-            )
+            work[rows, c : c + NB] -= dot(left, parts_ref[3 * top : 3 * begin, c : c + NB])
 
     for k in range(STEPS):
         top, begin = k * NB, (k + 1) * NB
@@ -585,8 +582,8 @@
             solved = dot(lower, high) + dot(lower, low)
             work[top : top + NB, c : c + NB] = solved
             high, low = split(solved)
-            high_ref[top : top + NB, c : c + NB] = high
-            low_ref[top : top + NB, c : c + NB] = low
+            for n, part in enumerate((high, low, high)):
+                parts_ref[3 * top + n * NB : 3 * top + (n + 1) * NB, c : c + NB] = part
         raw.run(2)
         if begin < PAN:
 
@@ -651,7 +648,7 @@
                 deal(me, target).wait_send()
 
 
-PLAN = (12, 6, 10, 10, 5, 8, 8)
+PLAN = (18, 12, 10, 4, 4, 6, 6)
 VMEM = pl.BlockSpec(memory_space=pltpu.VMEM)
 SMEM = pl.BlockSpec(memory_space=pltpu.SMEM)
 
@@ -693,8 +690,7 @@
             pltpu.VMEM((PAN, NB), F32),
             pltpu.VMEM((PAN, NB), F32),
             pltpu.VMEM((PAN + WIDE, PAN + WIDE), F32),
-            pltpu.VMEM((PAN, PAN + WIDE), BF16),
-            pltpu.VMEM((PAN, PAN + WIDE), BF16),
+            pltpu.VMEM((3 * PAN, PAN + WIDE), BF16),
             pltpu.VMEM((NB, NB), F32),
             *[dma((GATHER_SEMS,))] * 6,
             dma((PROWS,)), dma((STEPS,)), dma((PROWS,)), dma((PROWS,)),

time: 122 us -> 117 us (0.959)
  Pallas kernels: 118 us -> 113 us
    pallas_call x1, Pallas kernels: 116 us -> 111 us  [factor(): pl.pallas_call(main_kernel, out_shape=shape(WIDE, WIDE), in_specs=[SMEM]...]
where the time goes in v3:
time: 117 us
  Pallas kernels  113 us (97%)
  local copies, waits for them, and re-layouts  3.91 us (3%)
    pallas_call x1, Pallas kernels, factor(): pl.pallas_call(main_kernel, out_shape=shape(WIDE, WIDE), in_specs=[SMEM]...  111 us
    unnamed x5, local copies, waits for them, and re-layouts  3.91 us

profile of v3, /device:TPU:321, one launch (start us, length us, event | category | flops | bytes accessed | tf_op | source)
XLA Modules:
  0.0 116.7 jit_solution(6122613055365405178)
XLA Ops:
  0.0 0.0 copy-start.1
  0.0 0.1 pad_add_fusion.coord
  0.1 0.6 copy-done.1
  0.7 2.0 %shard_map.37 = (s32[8,256]{1,0:T(8,128)S(1)}, s32[8,128]{1,0:T(8,128)S(1)}, f32[1024,1]{1,0:T(8,128)S(1)}, f32[8,128]{1,0:T(8,128)S(1)}) custom-call(s32[2]{0:T(128)S(1)} %pad_add_fusion.coord, s32[4,256]{1,0:T(4,128)S(1)} %copy-done.1), custom_call_target="tpu_custom_call" | custom-call | tf_op jit(solution)/shard_map/pallas_call | solution.py:661
  2.7 0.0 copy-start
  2.7 1.0 copy-done
  3.7 110.7 %shard_map.38 = f32[512,512]{1,0:T(8,128)} custom-call(s32[8,256]{1,0:T(8,128)S(1)} %get-tuple-element.9.source_ref, s32[8,128]{1,0:T(8,128)S(1)} %get-tuple-element.10.slot_ref, f32[512,512]{1,0:T(8,128)} %a_ref.1, f32[1024,1]{1,0:T(8,128)S(1)} %get-tuple-element.11.local_ref, f32[8,128]{1,0:T(8,128)S(1)} %get-tuple-element.12.lanes_ref, ...), custom_call_target="tpu_custom_call" | custom-call | tf_op jit(solution)/shard_map/pallas_call | solution.py:678
  114.4 2.3 %copy.5 = f32[512,512]{1,0:T(8,128)} copy(f32[512,512]{1,0:T(8,128)} %shard_map.38) | data formatting | bytes 2097152
Async XLA Ops:
  0.0 0.7 copy-start.1
  2.7 1.0 copy-start
